TPU v7x, 32 devices: a whole 2x2x4 slice. The times are simulated.
32 devices in a mesh: grid: 4 (over z), snap: 8 (over y, x, core).
Axes of the slice: x: 2, y: 2, z: 4, core: 2. Of those that a mesh axis runs over, the one named last changes fastest.
Arguments:
- snapshots: bfloat16 [8192, 16384], P('grid', 'snap'), may hold values from -6 to 6
- test_matrix: bfloat16 [128, 8192], P(None, 'grid'), may hold values from -0.0625 to 0.0625
- leaf_pivots: int32 [8, 128], P('snap'), may hold values from 0 to 2047, as said below
- leaf_inverse: float32 [8, 128, 128], P('snap'), as said below
- merge_pivots: int32 [7, 128], replicated, may hold values from 0 to 255, as said below
- merge_inverse: float32 [7, 128, 128], replicated, as said below
- skeleton_ids: int32 [128], replicated, may hold values from 0 to 16383, as said below
Outputs:
- skeleton: bfloat16 [8192, 128], P('grid')
- coefficients: bfloat16 [128, 16384], P(None, 'snap')
Inputs may be any that keep to these rules, and one draw needn't show every extreme that they name: `leaf_pivots`: each row holds 128 distinct column numbers. `merge_pivots`: each row holds 128 distinct numbers. `skeleton_ids`: the ids that the tree keeps at node 1: leaf b starts with b * 2048 + leaf_pivots[b], each node keeps positions merge_pivots[n - 1] of its children's lists side by side. `leaf_inverse`: upper triangular with a positive diagonal. `merge_inverse`: upper triangular with a positive diagonal.
All inputs are finite; a program needn't handle non-finite values.
Results may differ from a plain program's by a relative error of at most 0.001.
Values may be sent and summed in bfloat16 or wider, within the bound.
A program may use at most 64 MiB of HBM per device.

v0:
```python
import jax
import jax.numpy as jnp
from jax import lax
from jax.sharding import PartitionSpec as P

PRECISE = lax.Precision.HIGHEST


def swapped(value, axis, bit):
    mask = 2**bit
    pairs = [(source, source ^ mask) for source in range(lax.axis_size(axis))]
    return lax.ppermute(value, axis, pairs)


def coefficient_block(kept_cols, stacked, picker, inverse):
    projected = jnp.dot(kept_cols.T, stacked, precision=PRECISE)
    coeffs = jnp.dot(inverse, projected, precision=PRECISE)
    chosen_mask = jnp.sum(picker, axis=1)
    return coeffs * (1.0 - chosen_mask)[None, :] + picker.T


def identify(stacked, pivots, inverse):
    picker = (jnp.arange(stacked.shape[1], dtype=jnp.int32)[:, None] == pivots[None, :]).astype(
        jnp.float32
    )
    kept_cols = jnp.dot(stacked, picker, precision=PRECISE)
    return (kept_cols, coefficient_block(kept_cols, stacked, picker, inverse))


def per_device(
    snapshots, test_matrix, leaf_pivots, leaf_inverse, merge_pivots, merge_inverse, skeleton_ids
):
    kept_count = test_matrix.shape[0]
    local_width = snapshots.shape[1]
    partial_value = jnp.dot(test_matrix, snapshots, preferred_element_type=jnp.float32)
    pivots = leaf_pivots[0]
    inverse = leaf_inverse[0]
    sketch = lax.psum(partial_value, "grid")
    kept_cols, leaf_coeffs = identify(sketch, pivots, inverse)
    blocks = lax.axis_size("snap")
    levels = blocks.bit_length() - 1
    block_index = lax.axis_index("snap")
    composed = jnp.eye(kept_count, dtype=jnp.float32)
    candidates = kept_cols
    for tree_level in range(levels):
        sibling = swapped(candidates, "snap", tree_level)
        which_side = block_index // 2**tree_level % 2
        lower_child = jnp.where(which_side == 0, candidates, sibling)
        upper_child = jnp.where(which_side == 0, sibling, candidates)
        stacked = jnp.concatenate([lower_child, upper_child], axis=1)
        node_row = blocks // 2 ** (tree_level + 1) - 1 + block_index // 2 ** (tree_level + 1)
        node_pivots = lax.dynamic_index_in_dim(merge_pivots, node_row, 0, keepdims=False)
        node_inverse = lax.dynamic_index_in_dim(merge_inverse, node_row, 0, keepdims=False)
        candidates, node_coeffs = identify(stacked, node_pivots, node_inverse)
        portion = lax.dynamic_slice_in_dim(node_coeffs, which_side * kept_count, kept_count, 1)
        composed = jnp.dot(portion, composed, precision=PRECISE)
    mapped = jnp.dot(composed, leaf_coeffs, precision=PRECISE).astype(jnp.bfloat16)
    local_cols = skeleton_ids - block_index * local_width
    inside = (local_cols >= 0) & (local_cols < local_width)
    clipped = jnp.clip(local_cols, 0, local_width - 1)
    picked = jnp.where(
        inside[None, :], jnp.take(snapshots, clipped, axis=1), jnp.zeros((), jnp.bfloat16)
    )
    skeleton = lax.psum(picked, "snap").astype(jnp.float32).astype(jnp.bfloat16)
    return (skeleton, mapped)


def solution(mesh):
    return jax.shard_map(
        per_device,
        mesh=mesh,
        in_specs=(
            P("grid", "snap"),
            P(None, "grid"),
            P("snap", None),
            P("snap", None, None),
            P(),
            P(),
            P(),
        ),
        out_specs=(P("grid", None), P(None, "snap")),
        check_vma=False,
    )
```

profile of v0, /device:TPU:0, one launch (start us, length us, event | category | flops | bytes accessed | tf_op | source)
XLA Modules:
  0.0 164.8 jit_solution(3252012088099845188)
XLA Ops:
  7.2 12.4 %copy.11 = bf16[2048,2048]{0,1:T(8,128)(2,1)} copy(bf16[2048,2048]{1,0:T(8,128)(2,1)} %param.7) | data formatting | bytes 16777216 | tf_op args[0]
  19.6 5.9 %gather_fusion = bf16[128,2048]{1,0:T(8,128)(2,1)S(1)} fusion(bf16[2048,2048]{0,1:T(8,128)(2,1)} %copy.11, s32[1024]{0:T(1024)S(1)} %pad_clamp_fusion), kind=kCustom, calls=%fused_computation | custom fusion | bytes 1049088 | tf_op jit(solution)/shard_map/jit(_take)/gather | solution.py:62
  25.5 0.9 select_bitcast_fusion
  26.5 0.2 all-reduce.5.cloned.1.call-start
  26.8 5.7 %fusion.59 = f32[128,2048]{1,0:T(8,128)} fusion(bf16[128,2048]{1,0:T(8,128)(2,1)S(1)} %copy-done, bf16[2048,2048]{1,0:T(8,128)(2,1)} %param.7), kind=kOutput, calls=%fused_computation.96 | convolution fusion | flops 1073741824 | bytes 9961472 | tf_op jit(solution)/shard_map/dot_general | solution.py:35
  32.6 0.8 fusion.52
  33.4 0.1 convert_reduce_fusion.1
  33.9 0.2 convert_reduce_fusion
  34.1 49.8 %all-reduce.3.cloned.1.call-done = bf16[2048,128]{0,1:T(8,128)(2,1)} async-done(((bf16[2048,128]{0,1:T(8,128)(2,1)}), bf16[2048,128]{0,1:T(8,128)(2,1)}) %all-reduce.3.cloned.1.call-update) | async-done | bytes 524304 | tf_op jit(solution)/shard_map/psum | solution.py:64
  83.9 2.0 %copy.12 = bf16[2048,128]{1,0:T(8,128)(2,1)} copy(bf16[2048,128]{0,1:T(8,128)(2,1)} %all-reduce.3.cloned.1.call-done) | data formatting | bytes 1048576
  85.9 51.6 %all-reduce.5.cloned.1.call-done = f32[128,2048]{1,0:T(8,128)} async-done(((f32[128,2048]{1,0:T(8,128)}), f32[128,2048]{1,0:T(8,128)}) %all-reduce.5.cloned.1.call-update) | async-done | bytes 1048592 | tf_op jit(solution)/shard_map/psum | solution.py:38
  137.5 2.3 %fusion.2 = f32[128,128]{0,1:T(8,128)S(1)} fusion(f32[128,2048]{1,0:T(8,128)} %all-reduce.5.cloned.1.call-done, s32[128]{0:T(128)S(1)} %bitcast.42), kind=kOutput, calls=%fused_computation.8 | convolution fusion | flops 402915328 | bytes 1114624 | tf_op jit(solution)/shard_map/dot_general | solution.py:26
  139.8 0.1 collective-permute-start
  139.9 2.2 %fusion.60 = f32[128,2048]{1,0:T(8,128)S(1)} fusion(f32[128,128]{0,1:T(8,128)S(1)} %fusion.2, f32[128,2048]{1,0:T(8,128)} %all-reduce.5.cloned.1.call-done), kind=kOutput, calls=%fused_computation.97 | convolution fusion | flops 402653184 | bytes 2162688 | tf_op jit(solution)/shard_map/dot_general | solution.py:16
  142.1 2.0 %fusion.1 = f32[128,2048]{0,1:T(8,128)S(1)} fusion(f32[128,2048]{1,0:T(8,128)S(1)} %fusion.60, s32[128]{0:T(128)S(1)} %bitcast.43, f32[2048]{0:T(1024)S(1)} %broadcast_subtract_fusion, f32[1,128,128]{2,1,0:T(8,128)S(1)} %copy-done.1), kind=kOutput, calls=%fused_computation.3 | convolution fusion | flops 403701760 | bytes 2171392 | tf_op jit(solution)/shard_map/dot_general | solution.py:17
  144.2 0.3 fusion.6
  144.5 0.3 fusion.9
  144.7 1.5 collective-permute-start.1
  146.3 1.1 fusion.20
  147.4 0.2 fusion.11
  147.6 1.6 collective-permute-done.1
  149.3 0.3 fusion.5
  149.6 0.3 fusion.8
  149.8 1.5 collective-permute-start.2
  151.4 1.1 fusion.22
  152.5 0.3 fusion.14
  152.8 1.4 collective-permute-done.2
  154.2 0.3 fusion.4
  154.5 0.3 fusion.7
  154.8 1.1 fusion.24
  155.9 0.3 fusion.17
  156.2 1.8 %convolution_convert_fusion = bf16[128,2048]{1,0:T(8,128)(2,1)} fusion(f32[128,128]{1,0:T(8,128)S(1)} %fusion.17, f32[128,2048]{0,1:T(8,128)S(1)} %fusion.1), kind=kOutput, calls=%fused_computation.4 | convolution fusion | flops 402915328 | bytes 1638400 | tf_op jit(solution)/shard_map/dot_general | solution.py:57
  (25 shorter events, 0.5 us)
Async XLA Ops:
  7.2 19.6 %copy-start = (bf16[128,2048]{1,0:T(8,128)(2,1)S(1)}, bf16[128,2048]{1,0:T(8,128)(2,1)}, u32[]{:S(2)}) copy-start(bf16[128,2048]{1,0:T(8,128)(2,1)} %param.8) | copy-start | bytes 1572868
  7.2 76.7 %all-reduce.3.cloned.1.call-start = ((), (), s32[]{:S(2)}) async-start(), calls=%async_computation | async-start | bytes 1048576 | tf_op jit(solution)/shard_map/psum | solution.py:64
  7.2 12.4 %copy-start.3 = (s32[128]{0:T(128)S(1)}, s32[128]{0:T(128)}, u32[]{:S(2)}) copy-start(s32[128]{0:T(128)} %param.13) | copy-start | bytes 1540
  26.5 7.4 %copy-start.2 = (s32[1,128]{1,0:T(1,128)S(1)}, s32[1,128]{1,0:T(1,128)}, u32[]{:S(2)}) copy-start(s32[1,128]{1,0:T(1,128)} %param.9) | copy-start | bytes 1540
  26.5 115.6 %copy-start.1 = (f32[1,128,128]{2,1,0:T(8,128)S(1)}, f32[1,128,128]{2,1,0:T(8,128)}, u32[]{:S(2)}) copy-start(f32[1,128,128]{2,1,0:T(8,128)} %param.10) | copy-start | bytes 196612
  26.5 111.0 %all-reduce.5.cloned.1.call-start = ((), (), s32[]{:S(2)}) async-start(), calls=%async_computation.1 | async-start | bytes 2097152 | tf_op jit(solution)/shard_map/psum | solution.py:38
  139.8 4.3 %collective-permute-start = (f32[128,128]{0,1:T(8,128)S(1)}, f32[128,128]{0,1:T(8,128)S(1)}, u32[]{:S(2)}, u32[]{:S(2)}) collective-permute-start(f32[128,128]{0,1:T(8,128)S(1)} %fusion.2), channel_id=1, source_target_pairs={{0,1},{1,0},{2,3},{3,2},{4,5},{5,4},{6,7},{7,6},{8,9},{9,8},{10,11... | collective-permute-start | bytes 196616 | tf_op jit(solution)/shard_map/ppermute | solution.py:12
  144.7 4.5 %collective-permute-start.1 = (f32[128,128]{0,1:T(8,128)S(1)}, f32[128,128]{0,1:T(8,128)S(1)}, u32[]{:S(2)}, u32[]{:S(2)}) collective-permute-start(f32[128,128]{0,1:T(8,128)S(1)} %fusion.6), channel_id=1, source_target_pairs={{0,2},{1,3},{2,0},{3,1},{4,6},{5,7},{6,4},{7,5},{8,10},{9,11},{10,... | collective-permute-start | bytes 196616 | tf_op jit(solution)/shard_map/ppermute | solution.py:12
  149.8 4.3 %collective-permute-start.2 = (f32[128,128]{0,1:T(8,128)S(1)}, f32[128,128]{0,1:T(8,128)S(1)}, u32[]{:S(2)}, u32[]{:S(2)}) collective-permute-start(f32[128,128]{0,1:T(8,128)S(1)} %fusion.5), channel_id=1, source_target_pairs={{0,4},{1,5},{2,6},{3,7},{4,0},{5,1},{6,2},{7,3},{8,12},{9,13},{10,... | collective-permute-start | bytes 196616 | tf_op jit(solution)/shard_map/ppermute | solution.py:12
Sparse Core Ops, SparseCore 0:
  26.6 57.2 all-reduce.2
  86.4 51.1 all-reduce.4
where the time goes:
time: 166 us; the launch traced here: 165 us
  waiting for transfers between devices  104 us (63%)
  local copies, waits for them, and re-layouts  21.4 us (13%)
  matrix products  19.7 us (12%)
  between operations  14.4 us (9%)
  starting transfers between devices  3.45 us (2%)
    psum x1, waiting for transfers between devices, per_device(): sketch = lax.psum(partial_value, 'grid')  51.6 us
    psum x1, waiting for transfers between devices, per_device(): skeleton = lax.psum(picked, 'snap').astype(jnp.float32).astype(jnp.bfloat16)  49.8 us
    unnamed x10, local copies, waits for them, and re-layouts  14.4 us
    gather x1, local copies, waits for them, and re-layouts, per_device(): jnp.take(snapshots, clipped, axis=1)  5.9 us
    dot_general x1, matrix products, per_device(): jnp.dot(test_matrix, snapshots, preferred_element_type=jnp.float32)  5.67 us
    dot_general x4, matrix products, coefficient_block(): coeffs = jnp.dot(inverse, projected, precision=PRECISE)  5.27 us
  transfers between devices with their start and end apart: 5, of which 4 were waited for; matrix products, arithmetic and copies ran while one was open for 10% of the time, Pallas kernels for 0%

commit v1 on v0

v1 whole, which is shorter than its diff:
```python
import functools

import jax
import jax.numpy as jnp
from jax import lax
from jax.experimental import pallas as pl
from jax.experimental.pallas import tpu as pltpu
from jax.sharding import PartitionSpec as P

PRECISE = lax.Precision.HIGHEST
F32, BF16, I32, I16 = jnp.float32, jnp.bfloat16, jnp.int32, jnp.int16
TILE = 256
LIMIT = 32000.0


def precise_dot(a, b):
    return jnp.dot(a, b, precision=PRECISE, preferred_element_type=F32)


def split3(x):
    hi = x.astype(BF16)
    rest = x - hi.astype(F32)
    mid = rest.astype(BF16)
    lo = (rest - mid.astype(F32)).astype(BF16)
    return hi, mid, lo


def kernel(
    n, m, s_ref, t_ref, lp_ref, li_ref, mp_ref, mi_ref, ids_ref,
    skel_out, coef_out,
    sv, oh, spart, srs, sfull, kpart, krs, kzag, kall, cands, pbuf, mx, scale, q, rin, lin, rsum,
    lsum, w_s, c_s,
    load_sem, k_send, k_recv, g_send, g_recv, a_send, a_recv, s_send, s_recv, f_send, f_recv,
    mx_send, mx_recv, r_send, r_recv, l_send, l_recv,
):
    z = lax.axis_index("grid")
    b = lax.axis_index("snap")
    rank = t_ref.shape[0]
    rows, cols = sv.shape
    row_tiles, chunks = rows // TILE, cols // TILE
    per_group = chunks // 2
    krows = rank // n
    srows = rows // m
    levels = m.bit_length() - 1

    def remote(src, dst, send, recv, axis, target):
        return pltpu.make_async_remote_copy(
            src_ref=src, dst_ref=dst, send_sem=send, recv_sem=recv,
            device_id={axis: target}, device_id_type=pl.DeviceIdType.MESH,
        )

    def load(i):
        part = pl.ds(pl.multiple_of(i * TILE, TILE), TILE)
        return pltpu.make_async_copy(s_ref.at[part], sv.at[part], load_sem.at[i])

    for i in range(row_tiles):
        load(i).start()

    barrier = pltpu.get_barrier_semaphore()
    z_peers = [lax.rem(z + o, n) for o in range(1, n)]
    b_peers = [lax.rem(b + o, m) for o in range(1, m)]
    for d in z_peers:
        pl.semaphore_signal(barrier, inc=1, device_id={"grid": d}, device_id_type=pl.DeviceIdType.MESH)
    for d in b_peers:
        pl.semaphore_signal(barrier, inc=1, device_id={"snap": d}, device_id_type=pl.DeviceIdType.MESH)

    @pl.when(z == 0)
    def _():
        rin[...] = jnp.zeros_like(rin)

    @pl.when(z == n - 1)
    def _():
        lin[...] = jnp.zeros_like(lin)

    for g in range(2):
        mx[g, z] = jnp.zeros(mx.shape[2:], F32)

    local_ids = ids_ref[...] - b * cols
    picks = jnp.concatenate([local_ids, lp_ref[...]], axis=1)

    def fill(i, carry):
        base = pl.multiple_of(i * TILE, TILE)
        place = lax.broadcasted_iota(I32, (TILE, 2 * rank), 0) + base
        oh[pl.ds(base, TILE), :] = (place == picks).astype(F32).astype(BF16)
        return carry

    lax.fori_loop(0, chunks, fill, 0)

    def pick(i, kept):
        part = pl.ds(pl.multiple_of(i * TILE, TILE), TILE)
        load(i).wait()
        got = jnp.dot(sv[part, :], oh[...], preferred_element_type=F32).astype(BF16)
        spart[part, :] = got[:, :rank]
        return kept + jnp.dot(t_ref[:, part], got[:, rank:], preferred_element_type=F32)

    kept = lax.fori_loop(0, row_tiles, pick, jnp.zeros((rank, rank), F32))
    kpart[...] = kept.reshape(n, krows, rank)
    pl.semaphore_wait(barrier, n + m - 2)

    def k_copy(d, slot):
        return remote(kpart.at[d], krs.at[slot], k_send.at[d], k_recv.at[slot], "grid", d)

    def g_copy(d, slot):
        return remote(kzag.at[slot], kzag.at[slot], g_send.at[d], g_recv.at[slot], "grid", d)

    def a_copy(d, slot):
        return remote(kall.at[slot], kall.at[slot], a_send.at[d], a_recv.at[slot], "snap", d)

    def block(i):
        return pl.ds(pl.multiple_of(i * srows, 16), srows)

    def s_copy(d, slot):
        return remote(spart.at[block(d)], srs.at[slot], s_send.at[d], s_recv.at[slot], "snap", d)

    def f_copy(d, slot):
        return remote(
            sfull.at[block(slot)], sfull.at[block(slot)], f_send.at[d], f_recv.at[slot], "snap", d)

    def mx_copy(g, d, slot):
        return remote(mx.at[g, slot], mx.at[g, slot], mx_send.at[g, d], mx_recv.at[g, slot], "grid", d)

    for d in z_peers:
        k_copy(d, z).start()
    for d in b_peers:
        s_copy(d, b).start()

    def sketch(g):
        def one(i, carry):
            c = g * per_group + i
            part = pl.ds(pl.multiple_of(c * TILE, TILE), TILE)
            value = jnp.dot(t_ref[...], sv[:, part], preferred_element_type=F32)
            pbuf[c] = value
            mx[g, z, pl.ds(i, 1), :] = jnp.max(jnp.abs(value), axis=0, keepdims=True)
            return carry

        lax.fori_loop(0, per_group, one, 0)
        for d in z_peers:
            mx_copy(g, d, z).start()

    def quantise(g):
        for d in z_peers:
            mx_copy(g, d, d).wait_recv()
        top = mx[g, 0]
        for i in range(1, n):
            top = top + mx[g, i]
        top = jnp.maximum(top, 1e-30)
        scale[g] = top * (1.0 / LIMIT)
        inv = LIMIT / top
        for i in range(per_group):
            c = g * per_group + i
            q[c] = jnp.floor(pbuf[c] * inv[i:i + 1, :] + 0.5).astype(I32).astype(I16)

    def right_copy(c):
        return remote(rsum.at[c], rin.at[c], r_send.at[c], r_recv.at[c], "grid", lax.rem(z + 1, n))

    def left_copy(c):
        return remote(lsum.at[c], lin.at[c], l_send.at[c], l_recv.at[c], "grid", lax.rem(z + n - 1, n))

    def added(x, y):
        return (x.astype(I32) + y.astype(I32)).astype(I16)

    def go_right(c):
        @pl.when(z > 0)
        def _():
            right_copy(c).wait_recv()

        @pl.when(z < n - 1)
        def _():
            rsum[c] = added(rin[c], q[c])
            right_copy(c).start()

    def go_left(c):
        @pl.when(z < n - 1)
        def _():
            left_copy(c).wait_recv()

        @pl.when(z > 0)
        def _():
            lsum[c] = added(lin[c], q[c])
            left_copy(c).start()

    def flow(step):
        @pl.when(z < n // 2)
        def _():
            if step < chunks:
                go_right(step)
            if step > 0:
                go_left(step - 1)

        @pl.when(z >= n // 2)
        def _():
            if step < chunks:
                go_left(step)
            if step > 0:
                go_right(step - 1)

    sketch(0)
    for d in z_peers:
        k_copy(d, d).wait_recv()
    krs[z] = kpart[z]
    total = krs[0]
    for i in range(1, n):
        total = total + krs[i]
    kzag[z] = total
    for d in z_peers:
        g_copy(d, z).start()
    quantise(0)
    flow(0)
    sketch(1)
    for d in z_peers:
        g_copy(d, d).wait_recv()
    kall[b] = kzag[...]
    for d in b_peers:
        a_copy(d, b).start()
    flow(1)
    flow(2)

    for d in b_peers:
        s_copy(d, d).wait_recv()
    acc = spart[block(b), :].astype(F32)
    for d in b_peers:
        acc = acc + srs[d].astype(F32)
    sfull[block(b), :] = acc.astype(BF16)
    for d in b_peers:
        f_copy(d, b).start()
    flow(3)
    quantise(1)
    flow(4)

    for d in b_peers:
        a_copy(d, d).wait_recv()
    starts = [0]
    for level in range(levels):
        starts.append(starts[-1] + (m >> level))
    for i in range(m):
        cands[i] = kall[i].reshape(rank, rank)
    next_flow = 5
    for level in range(levels):
        nodes = m >> (level + 1)
        for j in range(nodes):
            stacked = jnp.concatenate(
                [cands[starts[level] + 2 * j], cands[starts[level] + 2 * j + 1]], axis=1)
            row = nodes - 1 + j
            picker = (
                lax.broadcasted_iota(I32, (2 * rank, rank), 0) == mp_ref[row:row + 1, :]
            ).astype(F32).astype(BF16)
            three = jnp.dot(
                jnp.concatenate(split3(stacked), axis=0), picker, preferred_element_type=F32)
            cands[starts[level + 1] + j] = (
                three[:rank] + three[rank:2 * rank]) + three[2 * rank:]
        if next_flow <= chunks:
            flow(next_flow)
            next_flow += 1
    composed = None
    for level in range(levels):
        nodes = m >> (level + 1)
        j = b >> (level + 1)
        side = (b >> level) & 1
        chosen = cands[starts[level + 1] + j]
        child = cands[starts[level] + (b >> level)]
        row = nodes - 1 + j
        pivots = mp_ref[pl.ds(row, 1), :]
        picker_t = (
            lax.broadcasted_iota(I32, (rank, rank), 0) + side * rank == pivots
        ).astype(F32).T
        mask = jnp.sum(picker_t, axis=0, keepdims=True)
        inner = precise_dot(chosen.T, child)
        portion = precise_dot(mi_ref[row], inner) * (1.0 - mask) + picker_t
        composed = portion if composed is None else precise_dot(portion, composed)
        if next_flow <= chunks:
            flow(next_flow)
            next_flow += 1
    while next_flow <= chunks:
        flow(next_flow)
        next_flow += 1
    own = cands[b]
    weight = precise_dot(composed, precise_dot(li_ref[0], own.T))
    w_hi, w_mid, _ = split3(weight)
    w_s[...] = jnp.concatenate([w_hi, w_hi, w_mid, w_mid], axis=1)
    c_s[...] = composed.astype(BF16)

    pivot_col = jnp.broadcast_to(lp_ref[...].astype(F32), (rank, rank)).T[:, :1].astype(I32)
    for c in range(chunks):
        g, i = c // per_group, c % per_group
        hit = (lax.broadcasted_iota(I32, (rank, TILE), 1) + c * TILE == pivot_col).astype(F32)
        keep = 1.0 - jnp.sum(hit, axis=0, keepdims=True)
        sums = rin[c].astype(I32) + q[c].astype(I32) + lin[c].astype(I32)
        value = sums.astype(F32) * keep
        hi = value.astype(BF16)
        lo = (value - hi.astype(F32)).astype(BF16)
        mapped = jnp.dot(
            w_s[...], jnp.concatenate([hi, lo, hi, lo], axis=0), preferred_element_type=F32)
        unit = jnp.dot(c_s[...], hit.astype(BF16), preferred_element_type=F32)
        coef_out[:, c * TILE:(c + 1) * TILE] = (mapped * scale[g, i:i + 1, :] + unit).astype(BF16)

    for d in b_peers:
        f_copy(d, d).wait_recv()
    skel_out[...] = sfull[...]

    for d in z_peers:
        k_copy(d, z).wait_send()
        g_copy(d, z).wait_send()
        for g in range(2):
            mx_copy(g, d, z).wait_send()
    for d in b_peers:
        a_copy(d, b).wait_send()
        s_copy(d, b).wait_send()
        f_copy(d, b).wait_send()

    @pl.when(z < n - 1)
    def _():
        for c in range(chunks):
            right_copy(c).wait_send()

    @pl.when(z > 0)
    def _():
        for c in range(chunks):
            left_copy(c).wait_send()


def per_device(
    n, m, snapshots, test_matrix, leaf_pivots, leaf_inverse, merge_pivots, merge_inverse, skeleton_ids
):
    rank = test_matrix.shape[0]
    rows, cols = snapshots.shape
    chunks = cols // TILE
    krows, srows = rank // n, rows // m
    vmem = pl.BlockSpec(memory_space=pltpu.VMEM)
    dma = pltpu.SemaphoreType.DMA
    flow_shape = (chunks, rank, TILE)
    return pl.pallas_call(
        functools.partial(kernel, n, m),
        out_shape=(
            jax.ShapeDtypeStruct((rows, rank), BF16),
            jax.ShapeDtypeStruct((rank, cols), BF16),
        ),
        in_specs=[pl.BlockSpec(memory_space=pl.ANY)] + [vmem] * 6,
        out_specs=(vmem, vmem),
        scratch_shapes=[
            pltpu.VMEM((rows, cols), BF16),
            pltpu.VMEM((cols, 2 * rank), BF16),
            pltpu.VMEM((rows, rank), BF16),
            pltpu.VMEM((m, srows, rank), BF16),
            pltpu.VMEM((rows, rank), BF16),
            pltpu.VMEM((n, krows, rank), F32),
            pltpu.VMEM((n, krows, rank), F32),
            pltpu.VMEM((n, krows, rank), F32),
            pltpu.VMEM((m, n, krows, rank), F32),
            pltpu.VMEM((2 * m, rank, rank), F32),
            pltpu.VMEM(flow_shape, F32),
            pltpu.VMEM((2, n, chunks, TILE), F32),
            pltpu.VMEM((2, chunks, TILE), F32),
            pltpu.VMEM(flow_shape, I16),
            pltpu.VMEM(flow_shape, I16),
            pltpu.VMEM(flow_shape, I16),
            pltpu.VMEM(flow_shape, I16),
            pltpu.VMEM(flow_shape, I16),
            pltpu.VMEM((rank, 4 * rank), BF16),
            pltpu.VMEM((rank, rank), BF16),
            dma((rows // TILE,)),
            dma((n,)), dma((n,)), dma((n,)), dma((n,)),
            dma((m,)), dma((m,)), dma((m,)), dma((m,)), dma((m,)), dma((m,)),
            dma((2, n)), dma((2, n)),
            dma((chunks,)), dma((chunks,)), dma((chunks,)), dma((chunks,)),
        ],
        compiler_params=pltpu.CompilerParams(
            collective_id=0, has_side_effects=True, vmem_limit_bytes=48 * 2**20
        ),
    )(
        snapshots, test_matrix, leaf_pivots, leaf_inverse, merge_pivots, merge_inverse,
        skeleton_ids.reshape(1, rank),
    )


def solution(mesh):
    return jax.shard_map(
        functools.partial(per_device, mesh.shape["grid"], mesh.shape["snap"]),
        mesh=mesh,
        in_specs=(
            P("grid", "snap"),
            P(None, "grid"),
            P("snap", None),
            P("snap", None, None),
            P(),
            P(),
            P(),
        ),
        out_specs=(P("grid", None), P(None, "snap")),
        check_vma=False,
    )
```

time: 166 us -> 79.8 us (0.48)
  waiting for transfers between devices: 104 us -> 0 us
  Pallas kernels: 0 us -> 72.3 us
  matrix products: 19.7 us -> 0 us
  local copies, waits for them, and re-layouts: 21.4 us -> 6.48 us
  between operations: 14.4 us -> 0.65 us
  starting transfers between devices: 3.45 us -> 0 us
    psum x2 -> x0, waiting for transfers between devices: 101 us -> none  [the longest x1 51.6 us: per_device(): sketch = lax.psum(partial_value, 'grid')]
    pallas_call x0 -> x1, Pallas kernels: none -> 72.3 us  [per_device(): pl.pallas_call(functools.partial(kernel, n, m), out_shape=(jax.ShapeDtype...]
    dot_general x17 -> x0, matrix products: 19.7 us -> none  [the longest x1 5.67 us: per_device(): jnp.dot(test_matrix, snapshots, preferred_element_type=jnp.float32)]
    unnamed x10 -> x14, local copies, waits for them, and re-layouts: 14.4 us -> 6.48 us
    gather x1 -> x0, local copies, waits for them, and re-layouts: 5.9 us -> none  [per_device(): jnp.take(snapshots, clipped, axis=1)]
    ppermute x3 -> x0, starting transfers between devices: 3.19 us -> none  [swapped(): return lax.ppermute(value, axis, pairs)]
    ppermute x3 -> x0, waiting for transfers between devices: 3.06 us -> none  [swapped(): return lax.ppermute(value, axis, pairs)]
  transfers between devices with their start and end apart: 5 -> 0, of which waited for: 4 -> 0; matrix products, arithmetic and copies ran while one was open for 10% -> 0% of each run, Pallas kernels for 0% -> 0%
where the time goes in v1:
time: 79.8 us; the launch traced here: 79.4 us
  Pallas kernels  72.3 us (91%)
  local copies, waits for them, and re-layouts  6.48 us (8%)
    pallas_call x1, Pallas kernels, per_device(): pl.pallas_call(functools.partial(kernel, n, m), out_shape=(jax.ShapeDtype...  72.3 us
    unnamed x14, local copies, waits for them, and re-layouts  6.48 us

profile of v1, /device:TPU:0, one launch (start us, length us, event | category | flops | bytes accessed | tf_op | source)
XLA Modules:
  0.0 79.4 jit_solution(12671388432843448842)
XLA Ops:
  0.6 0.0 copy-start
  0.6 1.0 %copy-done = bf16[128,2048]{1,0:T(8,128)(2,1)S(1)} copy-done((bf16[128,2048]{1,0:T(8,128)(2,1)S(1)}, bf16[128,2048]{1,0:T(8,128)(2,1)}, u32[]{:S(2)}) %copy-start) | copy-done | bytes 524312
  1.7 0.0 copy-start.1
  1.7 1.0 %copy-done.1 = f32[7,128,128]{2,1,0:T(8,128)S(1)} copy-done((f32[7,128,128]{2,1,0:T(8,128)S(1)}, f32[7,128,128]{2,1,0:T(8,128)}, u32[]{:S(2)}) %copy-start.1) | copy-done | bytes 458776
  2.7 0.0 copy-start.2
  2.7 0.8 %copy-done.2 = f32[1,128,128]{2,1,0:T(8,128)S(1)} copy-done((f32[1,128,128]{2,1,0:T(8,128)S(1)}, f32[1,128,128]{2,1,0:T(8,128)}, u32[]{:S(2)}) %copy-start.2) | copy-done | bytes 65560
  3.5 0.0 copy-start.3
  3.5 0.7 copy-done.3
  4.2 0.0 copy-start.4
  4.2 0.7 copy-done.4
  4.9 0.0 copy-start.5
  4.9 0.7 copy-done.5
  5.5 72.3 %shard_map.86 = (bf16[2048,128]{1,0:T(8,128)(2,1)S(1)}, bf16[128,2048]{1,0:T(8,128)(2,1)S(1)}) custom-call(bf16[2048,2048]{1,0:T(8,128)(2,1)} %s_ref.1, bf16[128,2048]{1,0:T(8,128)(2,1)S(1)} %copy-done, s32[1,128]{1,0:T(1,128)S(1)} %copy-done.4, f32[1,128,128]{2,1,0:T(8,128)S(1)} %copy-done.2, s32[7,128]{1,0:T(8,128)S(1)} %copy-done.3, ...), custom_call_target="tpu_custom_call" | custom-call | tf_op jit(solution)/shard_map/pallas_call | solution.py:331
  77.9 0.8 %copy.11 = bf16[2048,128]{1,0:T(8,128)(2,1)} copy(bf16[2048,128]{1,0:T(8,128)(2,1)S(1)} %get-tuple-element.4) | data formatting | bytes 1048576
  78.7 0.8 copy.12
Async XLA Ops:
  0.6 1.0 %copy-start = (bf16[128,2048]{1,0:T(8,128)(2,1)S(1)}, bf16[128,2048]{1,0:T(8,128)(2,1)}, u32[]{:S(2)}) copy-start(bf16[128,2048]{1,0:T(8,128)(2,1)} %t_ref.1) | copy-start | bytes 1572868
  1.7 1.0 %copy-start.1 = (f32[7,128,128]{2,1,0:T(8,128)S(1)}, f32[7,128,128]{2,1,0:T(8,128)}, u32[]{:S(2)}) copy-start(f32[7,128,128]{2,1,0:T(8,128)} %mi_ref.1) | copy-start | bytes 1376260
  2.7 0.8 %copy-start.2 = (f32[1,128,128]{2,1,0:T(8,128)S(1)}, f32[1,128,128]{2,1,0:T(8,128)}, u32[]{:S(2)}) copy-start(f32[1,128,128]{2,1,0:T(8,128)} %li_ref.1) | copy-start | bytes 196612
  3.5 0.7 copy-start.3
  4.2 0.7 copy-start.4
  4.9 0.7 copy-start.5

commit v2 on v1

--- a/solution.py
+++ b/solution.py
@@ -11,6 +11,7 @@
 F32, BF16, I32, I16 = jnp.float32, jnp.bfloat16, jnp.int32, jnp.int16
 TILE = 256
 LIMIT = 32000.0
+LAG = 2
 
 
 def precise_dot(a, b):
@@ -26,8 +27,9 @@
 
 
 def kernel(
-    n, m, s_ref, t_ref, lp_ref, li_ref, mp_ref, mi_ref, ids_ref,
+    n, m, s_ref, t_hbm, lp_hbm, li_hbm, mp_hbm, mi_hbm, ids_hbm,
     skel_out, coef_out,
+    t_ref, lp_ref, li_ref, mp_ref, mi_ref, ids_ref, small_sem,
     sv, oh, spart, srs, sfull, kpart, krs, kzag, kall, cands, pbuf, mx, scale, q, rin, lin, rsum,
     lsum, w_s, c_s,
     load_sem, k_send, k_recv, g_send, g_recv, a_send, a_recv, s_send, s_recv, f_send, f_recv,
@@ -53,8 +55,18 @@
         part = pl.ds(pl.multiple_of(i * TILE, TILE), TILE)
         return pltpu.make_async_copy(s_ref.at[part], sv.at[part], load_sem.at[i])
 
+    small = [
+        pltpu.make_async_copy(src, dst, small_sem.at[i])
+        for i, (src, dst) in enumerate([
+            (ids_hbm, ids_ref), (lp_hbm, lp_ref), (t_hbm, t_ref), (mp_hbm, mp_ref),
+            (li_hbm, li_ref), (mi_hbm, mi_ref)])
+    ]
+    for copy in small[:3]:
+        copy.start()
     for i in range(row_tiles):
         load(i).start()
+    for copy in small[3:]:
+        copy.start()
 
     barrier = pltpu.get_barrier_semaphore()
     z_peers = [lax.rem(z + o, n) for o in range(1, n)]
@@ -75,6 +87,8 @@
     for g in range(2):
         mx[g, z] = jnp.zeros(mx.shape[2:], F32)
 
+    for copy in small[:2]:
+        copy.wait()
     local_ids = ids_ref[...] - b * cols
     picks = jnp.concatenate([local_ids, lp_ref[...]], axis=1)
 
@@ -85,6 +99,7 @@
         return carry
 
     lax.fori_loop(0, chunks, fill, 0)
+    small[2].wait()
 
     def pick(i, kept):
         part = pl.ds(pl.multiple_of(i * TILE, TILE), TILE)
@@ -160,39 +175,41 @@
         return (x.astype(I32) + y.astype(I32)).astype(I16)
 
     def go_right(c):
-        @pl.when(z > 0)
-        def _():
-            right_copy(c).wait_recv()
-
-        @pl.when(z < n - 1)
-        def _():
-            rsum[c] = added(rin[c], q[c])
-            right_copy(c).start()
+        right_copy(c).wait_recv()
+        rsum[c] = added(rin[c], q[c])
+        right_copy(c).start()
 
     def go_left(c):
-        @pl.when(z < n - 1)
-        def _():
-            left_copy(c).wait_recv()
-
-        @pl.when(z > 0)
-        def _():
-            lsum[c] = added(lin[c], q[c])
-            left_copy(c).start()
+        left_copy(c).wait_recv()
+        lsum[c] = added(lin[c], q[c])
+        left_copy(c).start()
+
+    def from_ends(g):
+        for c in range(g * per_group, (g + 1) * per_group):
+            @pl.when(z == 0)
+            def _():
+                rsum[c] = q[c]
+                right_copy(c).start()
+
+            @pl.when(z == n - 1)
+            def _():
+                lsum[c] = q[c]
+                left_copy(c).start()
 
     def flow(step):
-        @pl.when(z < n // 2)
+        @pl.when((z > 0) & (z < n // 2))
         def _():
             if step < chunks:
                 go_right(step)
-            if step > 0:
-                go_left(step - 1)
-
-        @pl.when(z >= n // 2)
+            if step >= LAG:
+                go_left(step - LAG)
+
+        @pl.when((z >= n // 2) & (z < n - 1))
         def _():
             if step < chunks:
                 go_left(step)
-            if step > 0:
-                go_right(step - 1)
+            if step >= LAG:
+                go_right(step - LAG)
 
     sketch(0)
     for d in z_peers:
@@ -205,15 +222,18 @@
     for d in z_peers:
         g_copy(d, z).start()
     quantise(0)
-    flow(0)
+    from_ends(0)
     sketch(1)
     for d in z_peers:
         g_copy(d, d).wait_recv()
     kall[b] = kzag[...]
     for d in b_peers:
         a_copy(d, b).start()
-    flow(1)
-    flow(2)
+    flow(0)
+    quantise(1)
+    from_ends(1)
+    for step in range(1, 5):
+        flow(step)
 
     for d in b_peers:
         s_copy(d, d).wait_recv()
@@ -223,9 +243,7 @@
     sfull[block(b), :] = acc.astype(BF16)
     for d in b_peers:
         f_copy(d, b).start()
-    flow(3)
-    quantise(1)
-    flow(4)
+    flow(5)
 
     for d in b_peers:
         a_copy(d, d).wait_recv()
@@ -234,7 +252,9 @@
         starts.append(starts[-1] + (m >> level))
     for i in range(m):
         cands[i] = kall[i].reshape(rank, rank)
-    next_flow = 5
+    next_flow = 6
+    for copy in small[3:]:
+        copy.wait()
     for level in range(levels):
         nodes = m >> (level + 1)
         for j in range(nodes):
@@ -248,7 +268,7 @@
                 jnp.concatenate(split3(stacked), axis=0), picker, preferred_element_type=F32)
             cands[starts[level + 1] + j] = (
                 three[:rank] + three[rank:2 * rank]) + three[2 * rank:]
-        if next_flow <= chunks:
+        if next_flow < chunks + LAG:
             flow(next_flow)
             next_flow += 1
     composed = None
@@ -267,10 +287,10 @@
         inner = precise_dot(chosen.T, child)
         portion = precise_dot(mi_ref[row], inner) * (1.0 - mask) + picker_t
         composed = portion if composed is None else precise_dot(portion, composed)
-        if next_flow <= chunks:
+        if next_flow < chunks + LAG:
             flow(next_flow)
             next_flow += 1
-    while next_flow <= chunks:
+    while next_flow < chunks + LAG:
         flow(next_flow)
         next_flow += 1
     own = cands[b]
@@ -278,6 +298,16 @@
     w_hi, w_mid, _ = split3(weight)
     w_s[...] = jnp.concatenate([w_hi, w_hi, w_mid, w_mid], axis=1)
     c_s[...] = composed.astype(BF16)
+
+    @pl.when(z == 0)
+    def _():
+        for c in range(chunks):
+            left_copy(c).wait_recv()
+
+    @pl.when(z == n - 1)
+    def _():
+        for c in range(chunks):
+            right_copy(c).wait_recv()
 
     pivot_col = jnp.broadcast_to(lp_ref[...].astype(F32), (rank, rank)).T[:, :1].astype(I32)
     for c in range(chunks):
@@ -334,9 +364,16 @@
             jax.ShapeDtypeStruct((rows, rank), BF16),
             jax.ShapeDtypeStruct((rank, cols), BF16),
         ),
-        in_specs=[pl.BlockSpec(memory_space=pl.ANY)] + [vmem] * 6,
+        in_specs=[pl.BlockSpec(memory_space=pl.ANY)] * 7,
         out_specs=(vmem, vmem),
         scratch_shapes=[
+            pltpu.VMEM(test_matrix.shape, BF16),
+            pltpu.VMEM(leaf_pivots.shape, I32),
+            pltpu.VMEM(leaf_inverse.shape, F32),
+            pltpu.VMEM(merge_pivots.shape, I32),
+            pltpu.VMEM(merge_inverse.shape, F32),
+            pltpu.VMEM((1, rank), I32),
+            dma((6,)),
             pltpu.VMEM((rows, cols), BF16),
             pltpu.VMEM((cols, 2 * rank), BF16),
             pltpu.VMEM((rows, rank), BF16),

time: 79.8 us -> 46.1 us (0.58)
  Pallas kernels: 72.3 us -> 38.7 us
    pallas_call x1, Pallas kernels: 72.3 us -> 38.7 us  [per_device(): pl.pallas_call(functools.partial(kernel, n, m), out_shape=(jax.ShapeDtype...]
where the time goes in v2:
time: 46.1 us; the launch traced here: 45.8 us
  Pallas kernels  38.7 us (84%)
  local copies, waits for them, and re-layouts  6.48 us (14%)
  between operations  0.65 us (1%)
    pallas_call x1, Pallas kernels, per_device(): pl.pallas_call(functools.partial(kernel, n, m), out_shape=(jax.ShapeDtype...  38.7 us
    unnamed x14, local copies, waits for them, and re-layouts  6.48 us

profile of v2, /device:TPU:0, one launch (start us, length us, event | category | flops | bytes accessed | tf_op | source)
XLA Modules:
  0.0 45.8 jit_solution(9175696876706243441)
XLA Ops:
  0.6 0.0 copy-start
  0.6 1.0 %copy-done = bf16[128,2048]{1,0:T(8,128)(2,1)S(1)} copy-done((bf16[128,2048]{1,0:T(8,128)(2,1)S(1)}, bf16[128,2048]{1,0:T(8,128)(2,1)}, u32[]{:S(2)}) %copy-start) | copy-done | bytes 524312
  1.7 0.0 copy-start.1
  1.7 1.0 %copy-done.1 = f32[7,128,128]{2,1,0:T(8,128)S(1)} copy-done((f32[7,128,128]{2,1,0:T(8,128)S(1)}, f32[7,128,128]{2,1,0:T(8,128)}, u32[]{:S(2)}) %copy-start.1) | copy-done | bytes 458776
  2.7 0.0 copy-start.2
  2.7 0.8 %copy-done.2 = f32[1,128,128]{2,1,0:T(8,128)S(1)} copy-done((f32[1,128,128]{2,1,0:T(8,128)S(1)}, f32[1,128,128]{2,1,0:T(8,128)}, u32[]{:S(2)}) %copy-start.2) | copy-done | bytes 65560
  3.5 0.0 copy-start.3
  3.5 0.7 %copy-done.3 = s32[7,128]{1,0:T(8,128)S(1)} copy-done((s32[7,128]{1,0:T(8,128)S(1)}, s32[7,128]{1,0:T(8,128)}, u32[]{:S(2)}) %copy-start.3) | copy-done | bytes 3608
  4.2 0.0 copy-start.4
  4.2 0.7 %copy-done.4 = s32[1,128]{1,0:T(1,128)S(1)} copy-done((s32[1,128]{1,0:T(1,128)S(1)}, s32[1,128]{1,0:T(1,128)}, u32[]{:S(2)}) %copy-start.4) | copy-done | bytes 536
  4.9 0.0 copy-start.5
  4.9 0.7 %copy-done.5 = s32[128]{0:T(128)S(1)} copy-done((s32[128]{0:T(128)S(1)}, s32[128]{0:T(128)}, u32[]{:S(2)}) %copy-start.5) | copy-done | bytes 536
  5.5 38.7 %shard_map.86 = (bf16[2048,128]{1,0:T(8,128)(2,1)S(1)}, bf16[128,2048]{1,0:T(8,128)(2,1)S(1)}) custom-call(bf16[2048,2048]{1,0:T(8,128)(2,1)} %s_ref.1, bf16[128,2048]{1,0:T(8,128)(2,1)S(1)} %copy-done, s32[1,128]{1,0:T(1,128)S(1)} %copy-done.4, f32[1,128,128]{2,1,0:T(8,128)S(1)} %copy-done.2, s32[7,128]{1,0:T(8,128)S(1)} %copy-done.3, ...), custom_call_target="tpu_custom_call" | custom-call | tf_op jit(solution)/shard_map/pallas_call | solution.py:361
  44.2 0.8 %copy.11 = bf16[2048,128]{1,0:T(8,128)(2,1)} copy(bf16[2048,128]{1,0:T(8,128)(2,1)S(1)} %get-tuple-element.4) | data formatting | bytes 1048576
  45.0 0.8 %copy.12 = bf16[128,2048]{1,0:T(8,128)(2,1)} copy(bf16[128,2048]{1,0:T(8,128)(2,1)S(1)} %get-tuple-element.5) | data formatting | bytes 1048576
Async XLA Ops:
  0.6 1.0 %copy-start = (bf16[128,2048]{1,0:T(8,128)(2,1)S(1)}, bf16[128,2048]{1,0:T(8,128)(2,1)}, u32[]{:S(2)}) copy-start(bf16[128,2048]{1,0:T(8,128)(2,1)} %t_hbm.1) | copy-start | bytes 1572868
  1.7 1.0 %copy-start.1 = (f32[7,128,128]{2,1,0:T(8,128)S(1)}, f32[7,128,128]{2,1,0:T(8,128)}, u32[]{:S(2)}) copy-start(f32[7,128,128]{2,1,0:T(8,128)} %mi_hbm.1) | copy-start | bytes 1376260
  2.7 0.8 %copy-start.2 = (f32[1,128,128]{2,1,0:T(8,128)S(1)}, f32[1,128,128]{2,1,0:T(8,128)}, u32[]{:S(2)}) copy-start(f32[1,128,128]{2,1,0:T(8,128)} %li_hbm.1) | copy-start | bytes 196612
  3.5 0.7 %copy-start.3 = (s32[7,128]{1,0:T(8,128)S(1)}, s32[7,128]{1,0:T(8,128)}, u32[]{:S(2)}) copy-start(s32[7,128]{1,0:T(8,128)} %mp_hbm.1) | copy-start | bytes 10756
  4.2 0.7 %copy-start.4 = (s32[1,128]{1,0:T(1,128)S(1)}, s32[1,128]{1,0:T(1,128)}, u32[]{:S(2)}) copy-start(s32[1,128]{1,0:T(1,128)} %lp_hbm.1) | copy-start | bytes 1540
  4.9 0.7 %copy-start.5 = (s32[128]{0:T(128)S(1)}, s32[128]{0:T(128)}, u32[]{:S(2)}) copy-start(s32[128]{0:T(128)} %param.13) | copy-start | bytes 1540

commit v3 on v2

--- a/solution.py
+++ b/solution.py
@@ -12,6 +12,7 @@
 TILE = 256
 LIMIT = 32000.0
 LAG = 2
+GROUPS = 4
 
 
 def precise_dot(a, b):
@@ -30,9 +31,10 @@
     n, m, s_ref, t_hbm, lp_hbm, li_hbm, mp_hbm, mi_hbm, ids_hbm,
     skel_out, coef_out,
     t_ref, lp_ref, li_ref, mp_ref, mi_ref, ids_ref, small_sem,
-    sv, oh, spart, srs, sfull, kpart, krs, kzag, kall, cands, pbuf, mx, scale, q, rin, lin, rsum,
+    sv, oh, spart, lcols, shalf, srs, sfull, kpart, krs, kzag, kall, cpick, v_s, pbuf, mx, scale, q, rin, lin, rsum,
     lsum, w_s, c_s,
-    load_sem, k_send, k_recv, g_send, g_recv, a_send, a_recv, s_send, s_recv, f_send, f_recv,
+    load_sem, k_send, k_recv, g_send, g_recv, a_send, a_recv, h_send, h_recv, s_send, s_recv,
+    f_send, f_recv,
     mx_send, mx_recv, r_send, r_recv, l_send, l_recv,
 ):
     z = lax.axis_index("grid")
@@ -40,7 +42,7 @@
     rank = t_ref.shape[0]
     rows, cols = sv.shape
     row_tiles, chunks = rows // TILE, cols // TILE
-    per_group = chunks // 2
+    per_group = chunks // GROUPS
     krows = rank // n
     srows = rows // m
     levels = m.bit_length() - 1
@@ -84,7 +86,7 @@
     def _():
         lin[...] = jnp.zeros_like(lin)
 
-    for g in range(2):
+    for g in range(GROUPS):
         mx[g, z] = jnp.zeros(mx.shape[2:], F32)
 
     for copy in small[:2]:
@@ -101,14 +103,15 @@
     lax.fori_loop(0, chunks, fill, 0)
     small[2].wait()
 
-    def pick(i, kept):
-        part = pl.ds(pl.multiple_of(i * TILE, TILE), TILE)
-        load(i).wait()
+    wide = 2 * TILE
+    for i in range(rows // wide):
+        part = pl.ds(i * wide, wide)
+        load(2 * i).wait()
+        load(2 * i + 1).wait()
         got = jnp.dot(sv[part, :], oh[...], preferred_element_type=F32).astype(BF16)
         spart[part, :] = got[:, :rank]
-        return kept + jnp.dot(t_ref[:, part], got[:, rank:], preferred_element_type=F32)
-
-    kept = lax.fori_loop(0, row_tiles, pick, jnp.zeros((rank, rank), F32))
+        lcols[part, :] = got[:, rank:]
+    kept = jnp.dot(t_ref[...], lcols[...], preferred_element_type=F32)
     kpart[...] = kept.reshape(n, krows, rank)
     pl.semaphore_wait(barrier, n + m - 2)
 
@@ -118,37 +121,53 @@
     def g_copy(d, slot):
         return remote(kzag.at[slot], kzag.at[slot], g_send.at[d], g_recv.at[slot], "grid", d)
 
+    core, chip, half = b & 1, b >> 1, m // 2
+    mate = b ^ 1
+    chip_peers = [lax.rem(chip + o, half) * 2 + core for o in range(1, half)]
+
     def a_copy(d, slot):
         return remote(kall.at[slot], kall.at[slot], a_send.at[d], a_recv.at[slot], "snap", d)
 
-    def block(i):
-        return pl.ds(pl.multiple_of(i * srows, 16), srows)
+    def a_forward(slot):
+        return remote(kall.at[slot], kall.at[slot], a_send.at[slot ^ 1], a_recv.at[slot], "snap", mate)
+
+    def block(d):
+        place = (d & 1) * half + (d >> 1)
+        return pl.ds(pl.multiple_of(place * srows, 16), srows)
+
+    def side(which):
+        return pl.ds(pl.multiple_of(which * half * srows, 16), half * srows)
+
+    def h_copy(which):
+        return remote(spart.at[side(which)], shalf, h_send, h_recv, "snap", mate)
 
     def s_copy(d, slot):
-        return remote(spart.at[block(d)], srs.at[slot], s_send.at[d], s_recv.at[slot], "snap", d)
+        return remote(
+            spart.at[block(d)], srs.at[slot >> 1], s_send.at[d >> 1], s_recv.at[slot >> 1], "snap", d)
 
     def f_copy(d, slot):
         return remote(
             sfull.at[block(slot)], sfull.at[block(slot)], f_send.at[d], f_recv.at[slot], "snap", d)
 
+    def f_forward(slot):
+        return remote(
+            sfull.at[block(slot)], sfull.at[block(slot)], f_send.at[slot ^ 1], f_recv.at[slot],
+            "snap", mate)
+
     def mx_copy(g, d, slot):
         return remote(mx.at[g, slot], mx.at[g, slot], mx_send.at[g, d], mx_recv.at[g, slot], "grid", d)
 
     for d in z_peers:
         k_copy(d, z).start()
-    for d in b_peers:
-        s_copy(d, b).start()
+    h_copy(1 - core).start()
 
     def sketch(g):
-        def one(i, carry):
+        for i in range(per_group):
             c = g * per_group + i
-            part = pl.ds(pl.multiple_of(c * TILE, TILE), TILE)
-            value = jnp.dot(t_ref[...], sv[:, part], preferred_element_type=F32)
+            value = jnp.dot(
+                t_ref[...], sv[:, c * TILE:(c + 1) * TILE], preferred_element_type=F32)
             pbuf[c] = value
-            mx[g, z, pl.ds(i, 1), :] = jnp.max(jnp.abs(value), axis=0, keepdims=True)
-            return carry
-
-        lax.fori_loop(0, per_group, one, 0)
+            mx[g, z, i:i + 1, :] = jnp.max(jnp.abs(value), axis=0, keepdims=True)
         for d in z_peers:
             mx_copy(g, d, z).start()
 
@@ -211,106 +230,92 @@
             if step >= LAG:
                 go_right(step - LAG)
 
-    sketch(0)
-    for d in z_peers:
-        k_copy(d, d).wait_recv()
-    krs[z] = kpart[z]
-    total = krs[0]
-    for i in range(1, n):
-        total = total + krs[i]
-    kzag[z] = total
-    for d in z_peers:
-        g_copy(d, z).start()
-    quantise(0)
-    from_ends(0)
-    sketch(1)
-    for d in z_peers:
-        g_copy(d, d).wait_recv()
-    kall[b] = kzag[...]
-    for d in b_peers:
-        a_copy(d, b).start()
-    flow(0)
-    quantise(1)
-    from_ends(1)
-    for step in range(1, 5):
-        flow(step)
-
-    for d in b_peers:
-        s_copy(d, d).wait_recv()
-    acc = spart[block(b), :].astype(F32)
-    for d in b_peers:
-        acc = acc + srs[d].astype(F32)
-    sfull[block(b), :] = acc.astype(BF16)
-    for d in b_peers:
-        f_copy(d, b).start()
-    flow(5)
-
-    for d in b_peers:
-        a_copy(d, d).wait_recv()
-    starts = [0]
-    for level in range(levels):
-        starts.append(starts[-1] + (m >> level))
-    for i in range(m):
-        cands[i] = kall[i].reshape(rank, rank)
-    next_flow = 6
-    for copy in small[3:]:
-        copy.wait()
-    for level in range(levels):
-        nodes = m >> (level + 1)
-        for j in range(nodes):
-            stacked = jnp.concatenate(
-                [cands[starts[level] + 2 * j], cands[starts[level] + 2 * j + 1]], axis=1)
-            row = nodes - 1 + j
-            picker = (
-                lax.broadcasted_iota(I32, (2 * rank, rank), 0) == mp_ref[row:row + 1, :]
-            ).astype(F32).astype(BF16)
-            three = jnp.dot(
-                jnp.concatenate(split3(stacked), axis=0), picker, preferred_element_type=F32)
-            cands[starts[level + 1] + j] = (
-                three[:rank] + three[rank:2 * rank]) + three[2 * rank:]
-        if next_flow < chunks + LAG:
-            flow(next_flow)
-            next_flow += 1
-    composed = None
-    for level in range(levels):
-        nodes = m >> (level + 1)
-        j = b >> (level + 1)
-        side = (b >> level) & 1
-        chosen = cands[starts[level + 1] + j]
-        child = cands[starts[level] + (b >> level)]
-        row = nodes - 1 + j
-        pivots = mp_ref[pl.ds(row, 1), :]
-        picker_t = (
-            lax.broadcasted_iota(I32, (rank, rank), 0) + side * rank == pivots
-        ).astype(F32).T
-        mask = jnp.sum(picker_t, axis=0, keepdims=True)
-        inner = precise_dot(chosen.T, child)
-        portion = precise_dot(mi_ref[row], inner) * (1.0 - mask) + picker_t
-        composed = portion if composed is None else precise_dot(portion, composed)
-        if next_flow < chunks + LAG:
-            flow(next_flow)
-            next_flow += 1
-    while next_flow < chunks + LAG:
-        flow(next_flow)
-        next_flow += 1
-    own = cands[b]
-    weight = precise_dot(composed, precise_dot(li_ref[0], own.T))
-    w_hi, w_mid, _ = split3(weight)
-    w_s[...] = jnp.concatenate([w_hi, w_hi, w_mid, w_mid], axis=1)
-    c_s[...] = composed.astype(BF16)
-
-    @pl.when(z == 0)
-    def _():
-        for c in range(chunks):
+    def skeleton_half():
+        h_copy(core).wait_recv()
+        h_copy(1 - core).wait_send()
+        mine = side(core)
+        spart[mine, :] = (spart[mine, :].astype(F32) + shalf[...].astype(F32)).astype(BF16)
+        for d in chip_peers:
+            s_copy(d, b).start()
+
+    def skeleton_block():
+        acc = spart[block(b), :].astype(F32)
+        for d in chip_peers:
+            s_copy(d, d).wait_recv()
+            acc = acc + srs[d >> 1].astype(F32)
+        sfull[block(b), :] = acc.astype(BF16)
+        for d in chip_peers + [mate]:
+            f_copy(d, b).start()
+
+    def skeleton_forward():
+        for d in chip_peers:
+            f_copy(d, d).wait_recv()
+            f_forward(d).start()
+
+    def selections():
+        def row_of(level, j):
+            return mp_ref[pl.ds((m >> (level + 1)) - 1 + j, 1), :]
+
+        ids = [j * 2 * rank + mp_ref[m // 2 - 1 + j:m // 2 + j, :] for j in range(m // 2)]
+        for level in range(levels):
+            if level:
+                merged = []
+                for j in range(len(ids) // 2):
+                    both = jnp.concatenate([ids[2 * j], ids[2 * j + 1]], axis=1).astype(F32)
+                    picker = (
+                        lax.broadcasted_iota(I32, (2 * rank, rank), 0)
+                        == mp_ref[len(ids) // 2 - 1 + j:len(ids) // 2 + j, :]
+                    ).astype(F32)
+                    found = precise_dot(jnp.broadcast_to(both, (8, 2 * rank)), picker)
+                    merged.append(jnp.floor(found[:1] + 0.5).astype(I32))
+                ids = merged
+            mine = ids[0]
+            for j in range(1, len(ids)):
+                mine = jnp.where(b >> (level + 1) == j, ids[j], mine)
+            for i in range(m):
+                place = lax.broadcasted_iota(I32, (rank, rank), 0) + i * rank
+                cpick[i, :, level * rank:(level + 1) * rank] = (
+                    place == mine).astype(F32).astype(BF16)
+
+    def tree():
+        three = None
+        for i in range(m):
+            parts = jnp.concatenate(split3(kall[i].reshape(rank, rank)), axis=0)
+            found = jnp.dot(parts, cpick[i], preferred_element_type=F32)
+            three = found if three is None else three + found
+        chosen = (three[:rank] + three[rank:2 * rank]) + three[2 * rank:]
+        path = [kall[b].reshape(rank, rank)]
+        for level in range(levels):
+            path.append(chosen[:, level * rank:(level + 1) * rank])
+        portions = []
+        for level in range(levels):
+            row = (m >> (level + 1)) - 1 + (b >> (level + 1))
+            picker_t = (
+                lax.broadcasted_iota(I32, (rank, rank), 0) + ((b >> level) & 1) * rank
+                == mp_ref[pl.ds(row, 1), :]
+            ).astype(F32).T
+            mask = jnp.sum(picker_t, axis=0, keepdims=True)
+            inner = precise_dot(path[level + 1].T, path[level])
+            portions.append(precise_dot(mi_ref[row], inner) * (1.0 - mask) + picker_t)
+        top = portions[-1]
+        for level in range(levels - 2, 0, -1):
+            top = precise_dot(top, portions[level])
+        first = precise_dot(portions[0], v_s[...])
+        composed = precise_dot(top, portions[0]) if levels > 1 else top
+        weight = precise_dot(top, first) if levels > 1 else first
+        w_hi, w_mid, _ = split3(weight)
+        w_s[...] = jnp.concatenate([w_hi, w_hi, w_mid, w_mid], axis=1)
+        c_s[...] = composed.astype(BF16)
+
+    def finish(c):
+        @pl.when(z == 0)
+        def _():
             left_copy(c).wait_recv()
 
-    @pl.when(z == n - 1)
-    def _():
-        for c in range(chunks):
+        @pl.when(z == n - 1)
+        def _():
             right_copy(c).wait_recv()
 
-    pivot_col = jnp.broadcast_to(lp_ref[...].astype(F32), (rank, rank)).T[:, :1].astype(I32)
-    for c in range(chunks):
         g, i = c // per_group, c % per_group
         hit = (lax.broadcasted_iota(I32, (rank, TILE), 1) + c * TILE == pivot_col).astype(F32)
         keep = 1.0 - jnp.sum(hit, axis=0, keepdims=True)
@@ -323,19 +328,77 @@
         unit = jnp.dot(c_s[...], hit.astype(BF16), preferred_element_type=F32)
         coef_out[:, c * TILE:(c + 1) * TILE] = (mapped * scale[g, i:i + 1, :] + unit).astype(BF16)
 
-    for d in b_peers:
-        f_copy(d, d).wait_recv()
+    sketch(0)
+    sketch(1)
+    for d in z_peers:
+        k_copy(d, d).wait_recv()
+    krs[z] = kpart[z]
+    total = krs[0]
+    for i in range(1, n):
+        total = total + krs[i]
+    kzag[z] = total
+    for d in z_peers:
+        g_copy(d, z).start()
+    quantise(0)
+    from_ends(0)
+    sketch(2)
+    quantise(1)
+    from_ends(1)
+    sketch(3)
+    for copy in small[3:]:
+        copy.wait()
+    for d in z_peers:
+        g_copy(d, d).wait_recv()
+    kall[b] = kzag[...]
+    for d in chip_peers + [mate]:
+        a_copy(d, b).start()
+    flow(0)
+    quantise(2)
+    from_ends(2)
+    flow(1)
+    quantise(3)
+    from_ends(3)
+    skeleton_half()
+    flow(2)
+    selections()
+    v_s[...] = precise_dot(li_ref[0], kzag[...].reshape(rank, rank).T)
+    pivot_col = jnp.broadcast_to(lp_ref[...].astype(F32), (rank, rank)).T[:, :1].astype(I32)
+    flow(3)
+    for d in chip_peers:
+        a_copy(d, d).wait_recv()
+        a_forward(d).start()
+    flow(4)
+    skeleton_block()
+    flow(5)
+    a_copy(mate, mate).wait_recv()
+    for d in chip_peers:
+        a_copy(d, d ^ 1).wait_recv()
+    tree()
+    for step in range(6, chunks + LAG):
+        flow(step)
+        if step == 6:
+            skeleton_forward()
+            for c in range(step - LAG):
+                finish(c)
+        finish(step - LAG)
+    f_copy(mate, mate).wait_recv()
+    for d in chip_peers:
+        f_copy(d, d ^ 1).wait_recv()
     skel_out[...] = sfull[...]
 
     for d in z_peers:
         k_copy(d, z).wait_send()
         g_copy(d, z).wait_send()
-        for g in range(2):
+        for g in range(GROUPS):
             mx_copy(g, d, z).wait_send()
-    for d in b_peers:
+    for d in chip_peers:
+        s_copy(d, b).wait_send()
         a_copy(d, b).wait_send()
-        s_copy(d, b).wait_send()
         f_copy(d, b).wait_send()
+        a_forward(d).wait_send()
+        f_forward(d).wait_send()
+    a_copy(mate, b).wait_send()
+    f_copy(mate, b).wait_send()
 
     @pl.when(z < n - 1)
     def _():
@@ -377,16 +440,19 @@
             pltpu.VMEM((rows, cols), BF16),
             pltpu.VMEM((cols, 2 * rank), BF16),
             pltpu.VMEM((rows, rank), BF16),
-            pltpu.VMEM((m, srows, rank), BF16),
+            pltpu.VMEM((rows, rank), BF16),
+            pltpu.VMEM((rows // 2, rank), BF16),
+            pltpu.VMEM((m // 2, srows, rank), BF16),
             pltpu.VMEM((rows, rank), BF16),
             pltpu.VMEM((n, krows, rank), F32),
             pltpu.VMEM((n, krows, rank), F32),
             pltpu.VMEM((n, krows, rank), F32),
             pltpu.VMEM((m, n, krows, rank), F32),
-            pltpu.VMEM((2 * m, rank, rank), F32),
+            pltpu.VMEM((m, rank, rank * (m.bit_length() - 1)), BF16),
+            pltpu.VMEM((rank, rank), F32),
             pltpu.VMEM(flow_shape, F32),
-            pltpu.VMEM((2, n, chunks, TILE), F32),
-            pltpu.VMEM((2, chunks, TILE), F32),
+            pltpu.VMEM((GROUPS, n, 8, TILE), F32),
+            pltpu.VMEM((GROUPS, 8, TILE), F32),
             pltpu.VMEM(flow_shape, I16),
             pltpu.VMEM(flow_shape, I16),
             pltpu.VMEM(flow_shape, I16),
@@ -396,12 +462,12 @@
             pltpu.VMEM((rank, rank), BF16),
             dma((rows // TILE,)),
             dma((n,)), dma((n,)), dma((n,)), dma((n,)),
-            dma((m,)), dma((m,)), dma((m,)), dma((m,)), dma((m,)), dma((m,)),
-            dma((2, n)), dma((2, n)),
+            dma((m,)), dma((m,)), dma, dma, dma((m // 2,)), dma((m // 2,)), dma((m,)), dma((m,)),
+            dma((GROUPS, n)), dma((GROUPS, n)),
             dma((chunks,)), dma((chunks,)), dma((chunks,)), dma((chunks,)),
         ],
         compiler_params=pltpu.CompilerParams(
-            collective_id=0, has_side_effects=True, vmem_limit_bytes=48 * 2**20
+            collective_id=0, has_side_effects=True, vmem_limit_bytes=64 * 2**20
         ),
     )(
         snapshots, test_matrix, leaf_pivots, leaf_inverse, merge_pivots, merge_inverse,

time: 46.1 us -> 50.4 us (1.093)
  Pallas kernels: 38.7 us -> 45.8 us
  local copies, waits for them, and re-layouts: 6.48 us -> 3.75 us
    pallas_call x1, Pallas kernels: 38.7 us -> 45.8 us  [per_device(): pl.pallas_call(functools.partial(kernel, n, m), out_shape=(jax.ShapeDtype...]
    unnamed x14 -> x2, local copies, waits for them, and re-layouts: 6.48 us -> 3.75 us
where the time goes in v3:
time: 50.4 us; the launch traced here: 50.2 us
  Pallas kernels  45.8 us (91%)
  local copies, waits for them, and re-layouts  3.75 us (7%)
  between operations  0.64 us (1%)
    pallas_call x1, Pallas kernels, per_device(): pl.pallas_call(functools.partial(kernel, n, m), out_shape=(jax.ShapeDtype...  45.8 us
    unnamed x2, local copies, waits for them, and re-layouts  3.75 us

profile of v3, /device:TPU:0, one launch (start us, length us, event | category | flops | bytes accessed | tf_op | source)
XLA Modules:
  0.0 50.2 jit_solution(18105790213464920952)
XLA Ops:
  0.6 45.8 %shard_map.86 = (bf16[2048,128]{1,0:T(8,128)(2,1)}, bf16[128,2048]{1,0:T(8,128)(2,1)}) custom-call(bf16[2048,2048]{1,0:T(8,128)(2,1)} %s_ref.1, bf16[128,2048]{1,0:T(8,128)(2,1)} %t_hbm.1, s32[1,128]{1,0:T(1,128)} %lp_hbm.1, f32[1,128,128]{2,1,0:T(8,128)} %li_hbm.1, s32[7,128]{1,0:T(8,128)} %mp_hbm.1, f32[7,128,128]{2,1,0:T(8,128)} %mi_hbm.1, s32[1,128]{1,0:T(1,128)} %bitcast.1), custom_call_target="tpu_custom_call" | custom-call | tf_op jit(solution)/shard_map/pallas_call | solution.py:424
  46.5 1.9 %copy.11 = bf16[2048,128]{1,0:T(8,128)(2,1)} copy(bf16[2048,128]{1,0:T(8,128)(2,1)} %get-tuple-element.4) | data formatting | bytes 1048576
  48.3 1.9 %copy.12 = bf16[128,2048]{1,0:T(8,128)(2,1)} copy(bf16[128,2048]{1,0:T(8,128)(2,1)} %get-tuple-element.5) | data formatting | bytes 1048576

commit v4 on v3

--- a/solution.py
+++ b/solution.py
@@ -31,7 +31,7 @@
     n, m, s_ref, t_hbm, lp_hbm, li_hbm, mp_hbm, mi_hbm, ids_hbm,
     skel_out, coef_out,
     t_ref, lp_ref, li_ref, mp_ref, mi_ref, ids_ref, small_sem,
-    sv, oh, spart, lcols, shalf, srs, sfull, kpart, krs, kzag, kall, cpick, v_s, pbuf, mx, scale, q, rin, lin, rsum,
+    sv, oh, spart, lcols, shalf, srs, sfull, kpart, krs, kzag, kall, cpick, kparts, inverse, v_s, pbuf, mx, scale, q, rin, lin, rsum,
     lsum, w_s, c_s,
     load_sem, k_send, k_recv, g_send, g_recv, a_send, a_recv, h_send, h_recv, s_send, s_recv,
     f_send, f_recv,
@@ -103,14 +103,15 @@
     lax.fori_loop(0, chunks, fill, 0)
     small[2].wait()
 
-    wide = 2 * TILE
-    for i in range(rows // wide):
-        part = pl.ds(i * wide, wide)
-        load(2 * i).wait()
-        load(2 * i + 1).wait()
+    def pick(i, carry):
+        part = pl.ds(pl.multiple_of(i * TILE, TILE), TILE)
+        load(i).wait()
         got = jnp.dot(sv[part, :], oh[...], preferred_element_type=F32).astype(BF16)
         spart[part, :] = got[:, :rank]
         lcols[part, :] = got[:, rank:]
+        return carry
+
+    lax.fori_loop(0, row_tiles, pick, 0)
     kept = jnp.dot(t_ref[...], lcols[...], preferred_element_type=F32)
     kpart[...] = kept.reshape(n, krows, rank)
     pl.semaphore_wait(barrier, n + m - 2)
@@ -162,12 +163,15 @@
     h_copy(1 - core).start()
 
     def sketch(g):
-        for i in range(per_group):
+        def one(i, carry):
             c = g * per_group + i
-            value = jnp.dot(
-                t_ref[...], sv[:, c * TILE:(c + 1) * TILE], preferred_element_type=F32)
+            part = pl.ds(pl.multiple_of(c * TILE, TILE), TILE)
+            value = jnp.dot(t_ref[...], sv[:, part], preferred_element_type=F32)
             pbuf[c] = value
-            mx[g, z, i:i + 1, :] = jnp.max(jnp.abs(value), axis=0, keepdims=True)
+            mx[g, z, pl.ds(i, 1), :] = jnp.max(jnp.abs(value), axis=0, keepdims=True)
+            return carry
+
+        lax.fori_loop(0, per_group, one, 0)
         for d in z_peers:
             mx_copy(g, d, z).start()
 
@@ -179,56 +183,74 @@
             top = top + mx[g, i]
         top = jnp.maximum(top, 1e-30)
         scale[g] = top * (1.0 / LIMIT)
-        inv = LIMIT / top
-        for i in range(per_group):
+        inverse[...] = LIMIT / top
+
+        def one(i, carry):
             c = g * per_group + i
-            q[c] = jnp.floor(pbuf[c] * inv[i:i + 1, :] + 0.5).astype(I32).astype(I16)
-
-    def right_copy(c):
-        return remote(rsum.at[c], rin.at[c], r_send.at[c], r_recv.at[c], "grid", lax.rem(z + 1, n))
-
-    def left_copy(c):
-        return remote(lsum.at[c], lin.at[c], l_send.at[c], l_recv.at[c], "grid", lax.rem(z + n - 1, n))
+            inv = inverse[pl.ds(i, 1), :]
+            q[c] = jnp.floor(pbuf[c] * inv + 0.5).astype(I32).astype(I16)
+            return carry
+
+        lax.fori_loop(0, per_group, one, 0)
+
+    def right_copy(c, src):
+        return remote(src.at[c], rin.at[c], r_send.at[c], r_recv.at[c], "grid", lax.rem(z + 1, n))
+
+    def left_copy(c, src):
+        return remote(src.at[c], lin.at[c], l_send.at[c], l_recv.at[c], "grid", lax.rem(z + n - 1, n))
 
     def added(x, y):
-        return (x.astype(I32) + y.astype(I32)).astype(I16)
+        return x + y
 
     def go_right(c):
-        right_copy(c).wait_recv()
+        right_copy(c, rsum).wait_recv()
         rsum[c] = added(rin[c], q[c])
-        right_copy(c).start()
+        right_copy(c, rsum).start()
 
     def go_left(c):
-        left_copy(c).wait_recv()
+        left_copy(c, lsum).wait_recv()
         lsum[c] = added(lin[c], q[c])
-        left_copy(c).start()
+        left_copy(c, lsum).start()
 
     def from_ends(g):
-        for c in range(g * per_group, (g + 1) * per_group):
+        def one(c, carry):
             @pl.when(z == 0)
             def _():
-                rsum[c] = q[c]
-                right_copy(c).start()
+                right_copy(c, q).start()
 
             @pl.when(z == n - 1)
             def _():
-                lsum[c] = q[c]
-                left_copy(c).start()
-
-    def flow(step):
+                left_copy(c, q).start()
+
+            return carry
+
+        lax.fori_loop(g * per_group, (g + 1) * per_group, one, 0)
+
+    def flow(step, carry=0):
         @pl.when((z > 0) & (z < n // 2))
         def _():
-            if step < chunks:
+            @pl.when(step < chunks)
+            def _():
                 go_right(step)
-            if step >= LAG:
+
+            @pl.when(step >= LAG)
+            def _():
                 go_left(step - LAG)
 
         @pl.when((z >= n // 2) & (z < n - 1))
         def _():
-            if step < chunks:
+            @pl.when(step < chunks)
+            def _():
                 go_left(step)
-            if step >= LAG:
+
+            @pl.when(step >= LAG)
+            def _():
                 go_right(step - LAG)
+
+        return carry
+
+    def flows(first, last):
+        lax.fori_loop(first, last, flow, 0)
 
     def skeleton_half():
         h_copy(core).wait_recv()
@@ -274,15 +296,14 @@
                 mine = jnp.where(b >> (level + 1) == j, ids[j], mine)
             for i in range(m):
                 place = lax.broadcasted_iota(I32, (rank, rank), 0) + i * rank
-                cpick[i, :, level * rank:(level + 1) * rank] = (
+                cpick[i * rank:(i + 1) * rank, level * rank:(level + 1) * rank] = (
                     place == mine).astype(F32).astype(BF16)
 
     def tree():
-        three = None
         for i in range(m):
-            parts = jnp.concatenate(split3(kall[i].reshape(rank, rank)), axis=0)
-            found = jnp.dot(parts, cpick[i], preferred_element_type=F32)
-            three = found if three is None else three + found
+            kparts[:, i * rank:(i + 1) * rank] = jnp.concatenate(
+                split3(kall[i].reshape(rank, rank)), axis=0)
+        three = jnp.dot(kparts[...], cpick[...], preferred_element_type=F32)
         chosen = (three[:rank] + three[rank:2 * rank]) + three[2 * rank:]
         path = [kall[b].reshape(rank, rank)]
         for level in range(levels):
@@ -307,16 +328,16 @@
         w_s[...] = jnp.concatenate([w_hi, w_hi, w_mid, w_mid], axis=1)
         c_s[...] = composed.astype(BF16)
 
-    def finish(c):
+    def finish(c, carry):
         @pl.when(z == 0)
         def _():
-            left_copy(c).wait_recv()
+            left_copy(c, lsum).wait_recv()
 
         @pl.when(z == n - 1)
         def _():
-            right_copy(c).wait_recv()
-
-        g, i = c // per_group, c % per_group
+            right_copy(c, rsum).wait_recv()
+
+        g, i = lax.div(c, per_group), lax.rem(c, per_group)
         hit = (lax.broadcasted_iota(I32, (rank, TILE), 1) + c * TILE == pivot_col).astype(F32)
         keep = 1.0 - jnp.sum(hit, axis=0, keepdims=True)
         sums = rin[c].astype(I32) + q[c].astype(I32) + lin[c].astype(I32)
@@ -326,7 +347,9 @@
         mapped = jnp.dot(
             w_s[...], jnp.concatenate([hi, lo, hi, lo], axis=0), preferred_element_type=F32)
         unit = jnp.dot(c_s[...], hit.astype(BF16), preferred_element_type=F32)
-        coef_out[:, c * TILE:(c + 1) * TILE] = (mapped * scale[g, i:i + 1, :] + unit).astype(BF16)
+        part = pl.ds(pl.multiple_of(c * TILE, TILE), TILE)
+        coef_out[:, part] = (mapped * scale[g, pl.ds(i, 1), :] + unit).astype(BF16)
+        return carry
 
     sketch(0)
     sketch(1)
@@ -352,35 +375,33 @@
     kall[b] = kzag[...]
     for d in chip_peers + [mate]:
         a_copy(d, b).start()
-    flow(0)
+    flows(0, 1)
     quantise(2)
     from_ends(2)
-    flow(1)
+    flows(1, 2)
     quantise(3)
     from_ends(3)
     skeleton_half()
-    flow(2)
+    flows(2, 3)
     selections()
     v_s[...] = precise_dot(li_ref[0], kzag[...].reshape(rank, rank).T)
     pivot_col = jnp.broadcast_to(lp_ref[...].astype(F32), (rank, rank)).T[:, :1].astype(I32)
-    flow(3)
+    flows(3, 4)
     for d in chip_peers:
         a_copy(d, d).wait_recv()
         a_forward(d).start()
-    flow(4)
+    flows(4, 5)
     skeleton_block()
-    flow(5)
+    flows(5, 6)
     a_copy(mate, mate).wait_recv()
     for d in chip_peers:
         a_copy(d, d ^ 1).wait_recv()
     tree()
-    for step in range(6, chunks + LAG):
-        flow(step)
-        if step == 6:
-            skeleton_forward()
-            for c in range(step - LAG):
-                finish(c)
-        finish(step - LAG)
+    flows(6, chunks)
+    skeleton_forward()
+    lax.fori_loop(0, chunks - LAG, finish, 0)
+    flows(chunks, chunks + LAG)
+    lax.fori_loop(chunks - LAG, chunks, finish, 0)
     f_copy(mate, mate).wait_recv()
     for d in chip_peers:
         f_copy(d, d ^ 1).wait_recv()
@@ -403,12 +424,12 @@
     @pl.when(z < n - 1)
     def _():
         for c in range(chunks):
-            right_copy(c).wait_send()
+            right_copy(c, rsum).wait_send()
 
     @pl.when(z > 0)
     def _():
         for c in range(chunks):
-            left_copy(c).wait_send()
+            left_copy(c, lsum).wait_send()
 
 
 def per_device(
@@ -448,7 +469,9 @@
             pltpu.VMEM((n, krows, rank), F32),
             pltpu.VMEM((n, krows, rank), F32),
             pltpu.VMEM((m, n, krows, rank), F32),
-            pltpu.VMEM((m, rank, rank * (m.bit_length() - 1)), BF16),
+            pltpu.VMEM((m * rank, rank * (m.bit_length() - 1)), BF16),
+            pltpu.VMEM((3 * rank, m * rank), BF16),
+            pltpu.VMEM((8, TILE), F32),
             pltpu.VMEM((rank, rank), F32),
             pltpu.VMEM(flow_shape, F32),
             pltpu.VMEM((GROUPS, n, 8, TILE), F32),
@@ -467,7 +490,7 @@
             dma((chunks,)), dma((chunks,)), dma((chunks,)), dma((chunks,)),
         ],
         compiler_params=pltpu.CompilerParams(
-            collective_id=0, has_side_effects=True, vmem_limit_bytes=64 * 2**20
+            collective_id=0, has_side_effects=True, vmem_limit_bytes=60 * 2**20
         ),
     )(
         snapshots, test_matrix, leaf_pivots, leaf_inverse, merge_pivots, merge_inverse,

time: 50.4 us -> 46.6 us (0.925)
  Pallas kernels: 45.8 us -> 42 us
    pallas_call x1, Pallas kernels: 45.8 us -> 42 us  [per_device(): pl.pallas_call(functools.partial(kernel, n, m), out_shape=(jax.ShapeDtype...]
where the time goes in v4:
time: 46.6 us; the launch traced here: 46.4 us
  Pallas kernels  42 us (90%)
  local copies, waits for them, and re-layouts  3.75 us (8%)
  between operations  0.64 us (1%)
    pallas_call x1, Pallas kernels, per_device(): pl.pallas_call(functools.partial(kernel, n, m), out_shape=(jax.ShapeDtype...  42 us
    unnamed x2, local copies, waits for them, and re-layouts  3.75 us

profile of v4, /device:TPU:0, one launch (start us, length us, event | category | flops | bytes accessed | tf_op | source)
XLA Modules:
  0.0 46.4 jit_solution(13526151879376850064)
XLA Ops:
  0.6 42.0 %shard_map.86 = (bf16[2048,128]{1,0:T(8,128)(2,1)}, bf16[128,2048]{1,0:T(8,128)(2,1)}) custom-call(bf16[2048,2048]{1,0:T(8,128)(2,1)} %s_ref.1, bf16[128,2048]{1,0:T(8,128)(2,1)} %t_hbm.1, s32[1,128]{1,0:T(1,128)} %lp_hbm.1, f32[1,128,128]{2,1,0:T(8,128)} %li_hbm.1, s32[7,128]{1,0:T(8,128)} %mp_hbm.1, f32[7,128,128]{2,1,0:T(8,128)} %mi_hbm.1, s32[1,128]{1,0:T(1,128)} %bitcast.1), custom_call_target="tpu_custom_call" | custom-call | tf_op jit(solution)/shard_map/pallas_call | solution.py:445
  42.7 1.9 %copy.11 = bf16[2048,128]{1,0:T(8,128)(2,1)} copy(bf16[2048,128]{1,0:T(8,128)(2,1)} %get-tuple-element.4) | data formatting | bytes 1048576
  44.5 1.9 %copy.12 = bf16[128,2048]{1,0:T(8,128)(2,1)} copy(bf16[128,2048]{1,0:T(8,128)(2,1)} %get-tuple-element.5) | data formatting | bytes 1048576

commit v5 on v4

--- a/solution.py
+++ b/solution.py
@@ -13,6 +13,7 @@
 LIMIT = 32000.0
 LAG = 2
 GROUPS = 4
+PIECES = 4
 
 
 def precise_dot(a, b):
@@ -105,15 +106,13 @@
 
     def pick(i, carry):
         part = pl.ds(pl.multiple_of(i * TILE, TILE), TILE)
-        load(i).wait()
         got = jnp.dot(sv[part, :], oh[...], preferred_element_type=F32).astype(BF16)
         spart[part, :] = got[:, :rank]
         lcols[part, :] = got[:, rank:]
         return carry
 
-    lax.fori_loop(0, row_tiles, pick, 0)
-    kept = jnp.dot(t_ref[...], lcols[...], preferred_element_type=F32)
-    kpart[...] = kept.reshape(n, krows, rank)
+    for i in range(row_tiles):
+        load(i).wait()
     pl.semaphore_wait(barrier, n + m - 2)
 
     def k_copy(d, slot):
@@ -157,10 +156,6 @@
 
     def mx_copy(g, d, slot):
         return remote(mx.at[g, slot], mx.at[g, slot], mx_send.at[g, d], mx_recv.at[g, slot], "grid", d)
-
-    for d in z_peers:
-        k_copy(d, z).start()
-    h_copy(1 - core).start()
 
     def sketch(g):
         def one(i, carry):
@@ -353,6 +348,19 @@
 
     sketch(0)
     sketch(1)
+    lax.fori_loop(0, row_tiles // 2, pick, 0)
+    quantise(0)
+    from_ends(0)
+    quantise(1)
+    from_ends(1)
+    lax.fori_loop(row_tiles // 2, row_tiles, pick, 0)
+    kept = jnp.dot(t_ref[...], lcols[...], preferred_element_type=F32)
+    kpart[...] = kept.reshape(n, krows, rank)
+    for d in z_peers:
+        k_copy(d, z).start()
+    h_copy(1 - core).start()
+    flows(0, 2)
+    sketch(2)
     for d in z_peers:
         k_copy(d, d).wait_recv()
     krs[z] = kpart[z]
@@ -362,12 +370,12 @@
     kzag[z] = total
     for d in z_peers:
         g_copy(d, z).start()
-    quantise(0)
-    from_ends(0)
-    sketch(2)
-    quantise(1)
-    from_ends(1)
     sketch(3)
+    flows(2, 3)
+    quantise(2)
+    from_ends(2)
+    quantise(3)
+    from_ends(3)
     for copy in small[3:]:
         copy.wait()
     for d in z_peers:
@@ -375,24 +383,17 @@
     kall[b] = kzag[...]
     for d in chip_peers + [mate]:
         a_copy(d, b).start()
-    flows(0, 1)
-    quantise(2)
-    from_ends(2)
-    flows(1, 2)
-    quantise(3)
-    from_ends(3)
+    flows(3, 4)
     skeleton_half()
-    flows(2, 3)
     selections()
     v_s[...] = precise_dot(li_ref[0], kzag[...].reshape(rank, rank).T)
     pivot_col = jnp.broadcast_to(lp_ref[...].astype(F32), (rank, rank)).T[:, :1].astype(I32)
-    flows(3, 4)
+    flows(4, 5)
     for d in chip_peers:
         a_copy(d, d).wait_recv()
         a_forward(d).start()
-    flows(4, 5)
+    flows(5, 6)
     skeleton_block()
-    flows(5, 6)
     a_copy(mate, mate).wait_recv()
     for d in chip_peers:
         a_copy(d, d ^ 1).wait_recv()
@@ -432,6 +433,19 @@
             left_copy(c, lsum).wait_send()
 
 
+def hand_over(skel_in, coef_in, skel_out, coef_out, sems):
+    copies = []
+    for k, (src, dst) in enumerate([(skel_in, skel_out), (coef_in, coef_out)]):
+        step = src.shape[0] // PIECES
+        for i in range(PIECES):
+            part = pl.ds(i * step, step)
+            copies.append(pltpu.make_async_copy(src.at[part], dst.at[part], sems.at[k, i]))
+    for copy in copies:
+        copy.start()
+    for copy in copies:
+        copy.wait()
+
+
 def per_device(
     n, m, snapshots, test_matrix, leaf_pivots, leaf_inverse, merge_pivots, merge_inverse, skeleton_ids
 ):
@@ -442,12 +456,13 @@
     vmem = pl.BlockSpec(memory_space=pltpu.VMEM)
     dma = pltpu.SemaphoreType.DMA
     flow_shape = (chunks, rank, TILE)
-    return pl.pallas_call(
+    shapes = (
+        jax.ShapeDtypeStruct((rows, rank), BF16),
+        jax.ShapeDtypeStruct((rank, cols), BF16),
+    )
+    outs = pl.pallas_call(
         functools.partial(kernel, n, m),
-        out_shape=(
-            jax.ShapeDtypeStruct((rows, rank), BF16),
-            jax.ShapeDtypeStruct((rank, cols), BF16),
-        ),
+        out_shape=shapes,
         in_specs=[pl.BlockSpec(memory_space=pl.ANY)] * 7,
         out_specs=(vmem, vmem),
         scratch_shapes=[
@@ -496,6 +511,15 @@
         snapshots, test_matrix, leaf_pivots, leaf_inverse, merge_pivots, merge_inverse,
         skeleton_ids.reshape(1, rank),
     )
+    anywhere = pl.BlockSpec(memory_space=pl.ANY)
+    return pl.pallas_call(
+        hand_over,
+        out_shape=shapes,
+        in_specs=[anywhere] * 2,
+        out_specs=(anywhere,) * 2,
+        scratch_shapes=[dma((2, PIECES))],
+        compiler_params=pltpu.CompilerParams(vmem_limit_bytes=60 * 2**20),
+    )(*outs)
 
 
 def solution(mesh):

time: 46.6 us -> 77.9 us (1.67)
  Pallas kernels: 42 us -> 77.1 us
  local copies, waits for them, and re-layouts: 3.75 us -> 0 us
    pallas_call x1 -> x2, Pallas kernels: 42 us -> 77.1 us  [the longest x1 44.1 us: per_device(): pl.pallas_call(functools.partial(kernel, n, m), out_shape=shapes, in_spec...]
    unnamed x2 -> x0, local copies, waits for them, and re-layouts: 3.75 us -> none
where the time goes in v5:
time: 77.9 us; the launch traced here: 77.7 us
  Pallas kernels  77.1 us (99%)
    pallas_call x1, Pallas kernels, per_device(): pl.pallas_call(functools.partial(kernel, n, m), out_shape=shapes, in_spec...  44.1 us
    pallas_call x1, Pallas kernels, per_device(): pl.pallas_call(hand_over, out_shape=shapes, in_specs=[anywhere] * 2, out_...  32.9 us

profile of v5, /device:TPU:0, one launch (start us, length us, event | category | flops | bytes accessed | tf_op | source)
XLA Modules:
  0.0 77.7 jit_solution(15772545422925312921)
XLA Ops:
  0.6 44.1 %shard_map.86 = (bf16[2048,128]{1,0:T(8,128)(2,1)}, bf16[128,2048]{1,0:T(8,128)(2,1)}) custom-call(bf16[2048,2048]{1,0:T(8,128)(2,1)} %s_ref.1, bf16[128,2048]{1,0:T(8,128)(2,1)} %t_hbm.1, s32[1,128]{1,0:T(1,128)} %lp_hbm.1, f32[1,128,128]{2,1,0:T(8,128)} %li_hbm.1, s32[7,128]{1,0:T(8,128)} %mp_hbm.1, f32[7,128,128]{2,1,0:T(8,128)} %mi_hbm.1, s32[1,128]{1,0:T(1,128)} %bitcast.1), custom_call_target="tpu_custom_call" | custom-call | tf_op jit(solution)/shard_map/pallas_call | solution.py:463
  44.8 32.9 %shard_map.87 = (bf16[2048,128]{1,0:T(8,128)(2,1)}, bf16[128,2048]{1,0:T(8,128)(2,1)}) custom-call(bf16[2048,128]{1,0:T(8,128)(2,1)} %get-tuple-element.4.skel_in, bf16[128,2048]{1,0:T(8,128)(2,1)} %get-tuple-element.5.coef_in), custom_call_target="tpu_custom_call" | custom-call | tf_op jit(solution)/shard_map/pallas_call | solution.py:515
